TPU v7x, 512 devices: a whole 4x4x16 slice. The times are simulated.
512 devices in a mesh: ctx: 16 (over y_lo, x, core), mp: 32 (over z, y_hi).
Axes of the slice: x: 4, y: 4 (y_hi: 2, y_lo: 2; y = y_hi * 2 + y_lo), z: 16, core: 2. Of those that a mesh axis runs over, the one named last changes fastest.
Arguments:
- queries: bfloat16 [16384, 4096], P('ctx', 'mp'), may hold values from -320 to 320
- keys_values: bfloat16 [16384, 2048], P('ctx', 'mp'), may hold values from -40 to 40
- query_taps: float32 [4, 4096], P(None, 'mp'), may hold values from -2.5 to 2.5
- pair_taps: float32 [4, 2048], P(None, 'mp'), may hold values from -2.5 to 2.5
- out_gain: float32 [4096], P('mp'), may hold values from 0.1 to 1.9
Outputs:
- head_outputs: bfloat16 [16384, 4096], P('ctx', 'mp')
All inputs are finite; a program needn't handle non-finite values.
Results may differ from a plain program's by a relative error of at most 0.012.
The roundings to bfloat16 on the way count: a program that leaves them out, or rounds other values in their place, can miss the bound.
Values may be sent and summed in bfloat16 or wider, within the bound.
No kernel may reach another device: no remote copies, remote signals or barrier semaphores. Data moves between devices by JAX's collectives and lax.ppermute only.
A program may use at most 64 MiB of HBM per device.

v0:
```python
import math
import jax
import jax.numpy as jnp
from jax import lax
from jax.sharding import PartitionSpec as P

HEAD_CHANNELS = 128
TAPS = 4
TRANSFORM_BLOCK = 128
KEEP = 16
NEGATIVE = -1e30
EPSILON = 1e-06


def shifted(value, axis, steps):
    count = lax.axis_size(axis)
    leading, last = (max(0, -steps), min(count, count - steps))
    return lax.ppermute(value, axis, [(source, source + steps) for source in range(leading, last)])


def from_partner(block, axis, apart):
    count = lax.axis_size(axis)
    route = []
    for low in range(count):
        high = low | 1 << apart
        if high != low and high < count:
            route += [(low, high), (high, low)]
    return lax.ppermute(block, axis, route)


def dct_table():
    frequency = jnp.arange(KEEP, dtype=jnp.float32)[:, None]
    offset = jnp.arange(TRANSFORM_BLOCK, dtype=jnp.float32)[None, :]
    table = jnp.cos(math.pi * (offset + 0.5) * frequency / TRANSFORM_BLOCK) * math.sqrt(
        2.0 / TRANSFORM_BLOCK
    )
    table = jnp.where(frequency == 0.0, table * math.sqrt(0.5), table)
    return table.astype(jnp.bfloat16)


def compress(values):
    blocks = values.reshape(values.shape[0] // TRANSFORM_BLOCK, TRANSFORM_BLOCK, values.shape[1])
    packed = jnp.einsum("jt,btc->bjc", dct_table(), blocks, preferred_element_type=jnp.float32)
    return packed.astype(jnp.bfloat16).reshape(-1, values.shape[1])


def causal_conv(history, values, weights):
    lead = weights.shape[0] - 1
    padded = jnp.concatenate([history, values], 0)
    length = values.shape[0]
    total = weights[0] * values.astype(jnp.float32)
    for shift in range(1, weights.shape[0]):
        total = total + weights[shift] * padded[lead - shift : lead - shift + length].astype(
            jnp.float32
        )
    return total.astype(jnp.bfloat16)


def local_state(query_heads, pairs, score_scale):
    entry_count = query_heads.shape[0] // TRANSFORM_BLOCK
    heads = query_heads.shape[1]
    scores = (
        jnp.einsum(
            "uxwi,umi->uxwm",
            query_heads.reshape(entry_count, TRANSFORM_BLOCK, heads, HEAD_CHANNELS),
            pairs[:, :HEAD_CHANNELS].reshape(entry_count, TRANSFORM_BLOCK, HEAD_CHANNELS),
            preferred_element_type=jnp.float32,
        )
        * score_scale
    )
    causal = (
        jnp.arange(TRANSFORM_BLOCK)[:, None, None] >= jnp.arange(TRANSFORM_BLOCK)[None, None, :]
    )
    scores = jnp.where(causal, scores, NEGATIVE)
    top = jnp.max(scores, -1)
    weights = jnp.where(causal, jnp.exp(scores - top[..., None]), 0.0)
    total = jnp.sum(weights, -1)
    summed = jnp.einsum(
        "cevo,coa->ceva",
        weights.astype(jnp.bfloat16),
        pairs[:, HEAD_CHANNELS:].reshape(entry_count, TRANSFORM_BLOCK, HEAD_CHANNELS),
        preferred_element_type=jnp.float32,
    )
    rows = entry_count * TRANSFORM_BLOCK
    return (
        top.reshape(rows, heads),
        total.reshape(rows, heads),
        summed.reshape(rows, heads, HEAD_CHANNELS),
    )


def attend(state, query_heads, query_blocks, keys, key_blocks, score_scale):
    top, total, summed = state
    entry_count = query_heads.shape[0]
    size = 512
    tops, totals, sums = ([], [], [])
    for begin in range(0, entry_count, size):
        part = query_heads[begin : begin + size]
        scores = (
            jnp.einsum(
                "qhd,kd->qhk", part, keys[:, :HEAD_CHANNELS], preferred_element_type=jnp.float32
            )
            * score_scale
        )
        seen = key_blocks[None, None, :] < query_blocks[begin : begin + size, None, None]
        scores = jnp.where(seen, scores, NEGATIVE)
        old_top = top[begin : begin + size]
        new_top = jnp.maximum(old_top, jnp.max(scores, -1))
        weights = jnp.where(seen, jnp.exp(scores - new_top[..., None]), 0.0)
        rescale = jnp.exp(old_top - new_top)
        totals.append(rescale * total[begin : begin + size] + jnp.sum(weights, -1))
        sums.append(
            rescale[..., None] * summed[begin : begin + size]
            + jnp.einsum(
                "qhk,kd->qhd",
                weights.astype(jnp.bfloat16),
                keys[:, HEAD_CHANNELS:],
                preferred_element_type=jnp.float32,
            )
        )
        tops.append(new_top)
    return (jnp.concatenate(tops, 0), jnp.concatenate(totals, 0), jnp.concatenate(sums, 0))


def per_device(queries, keys_values, query_taps, pair_taps, out_gain):
    rows = queries.shape[0]
    span_rows = rows // 2
    per_span = span_rows // TRANSFORM_BLOCK
    shards = lax.axis_size("ctx")
    place = lax.axis_index("ctx")
    member = lax.axis_index("mp")
    score_scale = 1.0 / math.sqrt(HEAD_CHANNELS)
    tail = TAPS - 1
    columns = queries.shape[1]
    first_tail = jnp.concatenate(
        [queries[span_rows - tail : span_rows], keys_values[span_rows - tail : span_rows]], 1
    )
    second_tail = jnp.concatenate([queries[rows - tail :], keys_values[rows - tail :]], 1)
    from_lower = shifted(first_tail, "ctx", 1)
    from_upper = shifted(second_tail, "ctx", -1)
    before_second = jnp.where(place == shards - 1, first_tail, from_upper)
    query_conv = jnp.concatenate(
        [
            causal_conv(from_lower[:, :columns], queries[:span_rows], query_taps),
            causal_conv(before_second[:, :columns], queries[span_rows:], query_taps),
        ],
        0,
    )
    pair_conv = jnp.concatenate(
        [
            causal_conv(from_lower[:, columns:], keys_values[:span_rows], pair_taps),
            causal_conv(before_second[:, columns:], keys_values[span_rows:], pair_taps),
        ],
        0,
    )
    width = keys_values.shape[1]
    rounds = (2 * HEAD_CHANNELS // width).bit_length() - 1

    def join(mine, other, bit):
        lower = member // 2**bit % 2 == 0
        return jnp.where(
            lower, jnp.concatenate([mine, other], 1), jnp.concatenate([other, mine], 1)
        )

    pairs = pair_conv
    packed = compress(pair_conv)
    for bit in range(rounds):
        other = from_partner(jnp.concatenate([pairs, packed], 0), "mp", bit)
        pairs = join(pairs, other[:rows], bit)
        packed = join(packed, other[rows:], bit)
    heads_here = columns // HEAD_CHANNELS
    query_heads = query_conv.reshape(rows, heads_here, HEAD_CHANNELS)
    own_rows = jnp.arange(rows)
    own_span = jnp.where(own_rows < span_rows, place, 2 * shards - 1 - place)
    query_blocks = own_span * per_span + own_rows % span_rows // TRANSFORM_BLOCK
    state = local_state(query_heads, pairs, score_scale)
    shard_rows = rows * KEEP // TRANSFORM_BLOCK
    half_rows = shard_rows // 2
    piece = lax.all_gather(packed, "ctx", axis=0, tiled=True)
    positions = jnp.arange(piece.shape[0])
    owner = positions // shard_rows
    within = positions % shard_rows
    span_index = jnp.where(within < half_rows, owner, 2 * shards - 1 - owner)
    key_blocks = span_index * per_span + within % half_rows // KEEP
    state = attend(state, query_heads, query_blocks, piece, key_blocks, score_scale)
    top, total, summed = state
    attended = summed / total[..., None]
    normed = attended * lax.rsqrt(jnp.mean(attended * attended, -1, keepdims=True) + EPSILON)
    return (normed.reshape(rows, columns) * out_gain).astype(jnp.bfloat16)


def solution(mesh):
    in_specs = (P("ctx", "mp"), P("ctx", "mp"), P(None, "mp"), P(None, "mp"), P("mp"))
    out_specs = P("ctx", "mp")
    return jax.shard_map(
        per_device, mesh=mesh, in_specs=in_specs, out_specs=out_specs, check_vma=False
    )
```

profile of v0, /device:TPU:1, one launch (start us, length us, event | category | flops | bytes accessed | tf_op | source)
XLA Modules:
  0.0 103.2 jit_solution(5550732140074275808)
XLA Ops:
  6.5 0.0 all-gather.2.cloned.1.call-start
  6.5 0.7 fusion.93
  7.2 0.8 fusion.95
  8.1 0.1 copy.40
  8.2 8.8 %collective-permute-start.1 = (bf16[3,192]{1,0:T(4,128)(2,1)S(1)}, bf16[3,192]{1,0:T(4,128)(2,1)S(1)}, u32[]{:S(2)}, u32[]{:S(2)}) collective-permute-start(bf16[3,192]{1,0:T(4,128)(2,1)S(1)} %pad_maximum_fusion.9), channel_id=1, source_target_pairs={{32,0},{64,32},{96,64},{128,96},{160,128},{192,160},{224,192},{256... | collective-permute-start | bytes 3464 | tf_op jit(solution)/shard_map/ppermute | solution.py:18
  17.0 0.9 fusion.94
  17.8 0.8 slice_bitcast_fusion.3
  18.7 0.1 copy.39
  18.8 0.0 collective-permute-done.1
  18.8 1.9 %collective-permute-start = (bf16[3,192]{1,0:T(4,128)(2,1)S(1)}, bf16[3,192]{1,0:T(4,128)(2,1)S(1)}, u32[]{:S(2)}, u32[]{:S(2)}) collective-permute-start(bf16[3,192]{1,0:T(4,128)(2,1)S(1)} %get-tuple-element.37), channel_id=1, source_target_pairs={{0,32},{32,64},{64,96},{96,128},{128,160},{160,192},{192,224},{224... | collective-permute-start | bytes 3464 | tf_op jit(solution)/shard_map/ppermute | solution.py:18
  20.8 0.1 copy.30
  20.9 1.0 collective-permute-done
  21.9 0.1 copy.29
  22.0 0.2 add_convert_fusion.3
  22.3 0.2 convolution_convert_fusion
  22.5 0.1 copy.32
  22.6 1.9 %collective-permute-start.2 = (bf16[1152,64]{0,1:T(8,128)(2,1)S(1)}, bf16[1152,64]{0,1:T(8,128)(2,1)S(1)}, u32[]{:S(2)}, u32[]{:S(2)}) collective-permute-start(bf16[1152,64]{0,1:T(8,128)(2,1)S(1)} %pad_maximum_fusion.2), channel_id=1, source_target_pairs={{0,1},{1,0},{2,3},{3,2},{4,5},{5,4},{6,7},{7,6},{8,9},{9,8},{10,11... | collective-permute-start | bytes 442376 | tf_op jit(solution)/shard_map/ppermute | solution.py:28
  24.5 0.8 slice_bitcast_fusion.7
  25.4 5.9 %collective-permute-done.2 = bf16[1152,64]{0,1:T(8,128)(2,1)S(1)} collective-permute-done((bf16[1152,64]{0,1:T(8,128)(2,1)S(1)}, bf16[1152,64]{0,1:T(8,128)(2,1)S(1)}, u32[]{:S(2)}, u32[]{:S(2)}) %collective-permute-start.2) | collective-permute-done | bytes 147488 | tf_op jit(solution)/shard_map/ppermute | solution.py:28
  31.3 0.1 maximum_select_fusion.1
  31.4 1.9 %collective-permute-start.3 = (bf16[1152,128]{0,1:T(8,128)(2,1)S(1)}, bf16[1152,128]{0,1:T(8,128)(2,1)S(1)}, u32[]{:S(2)}, u32[]{:S(2)}) collective-permute-start(bf16[1152,128]{0,1:T(8,128)(2,1)S(1)} %pad_maximum_fusion), channel_id=1, source_target_pairs={{0,2},{2,0},{1,3},{3,1},{4,6},{6,4},{5,7},{7,5},{8,10},{10,8},{9,1... | collective-permute-start | bytes 884744 | tf_op jit(solution)/shard_map/ppermute | solution.py:28
  33.4 1.0 fusion.92
  34.4 6.5 %collective-permute-done.3 = bf16[1152,128]{0,1:T(8,128)(2,1)S(1)} collective-permute-done((bf16[1152,128]{0,1:T(8,128)(2,1)S(1)}, bf16[1152,128]{0,1:T(8,128)(2,1)S(1)}, u32[]{:S(2)}, u32[]{:S(2)}) %collective-permute-start.3) | collective-permute-done | bytes 294944 | tf_op jit(solution)/shard_map/ppermute | solution.py:28
  40.9 0.6 maximum_select_fusion.2
  41.5 0.0 all-gather.2.cloned.1.call-update
  41.5 0.3 add_convert_fusion.1
  41.9 0.1 maximum_select_fusion
  42.0 0.2 copy.35
  42.2 0.2 copy.36
  42.4 0.3 fusion.99
  42.7 0.1 fusion.28
  42.9 0.3 fusion.30
  43.2 43.6 %all-gather.2.cloned.1.call-done = bf16[2048,256]{0,1:T(8,128)(2,1)} async-done(((bf16[128,256]{0,1:T(8,128)(2,1)}), bf16[2048,256]{0,1:T(8,128)(2,1)}) %all-gather.2.cloned.1.call-update) | async-done | bytes 1048592 | tf_op jit(solution)/shard_map/all_gather | solution.py:179
  86.8 0.0 copy-start.1
  86.8 2.0 %fusion = (f32[512]{0:T(512)S(1)}, f32[512,2048]{1,0:T(8,128)S(1)}) fusion(s32[2048]{0:T(1024)S(1)} %fusion.52, s32[512]{0:T(512)S(1)} %get-tuple-element.28, bf16[512,128]{1,0:T(8,128)(2,1)S(1)} %get-tuple-element.29, bf16[2048,256]{0,1:T(8,128)(2,1)} %all-gather.2.cloned.1.call-done), kind=kOutput, calls=%fused_computation.4 | convolution fusion | flops 272629248 | bytes 4861952 | tf_op jit(solution)/shard_map/qhd,kd->qhk/dot_general | solution.py:100
  88.8 0.0 copy-done.1
  88.9 2.1 %fusion.2 = (f32[512]{0:T(512)S(1)}, f32[512]{0:T(512)S(1)}, f32[512,2048]{1,0:T(8,128)S(1)}) fusion(f32[512,2048]{1,0:T(8,128)S(1)} %get-tuple-element.46, f32[512]{0:T(512)S(1)} %get-tuple-element.20, s32[2048]{0:T(1024)S(1)} %fusion.52, s32[512]{0:T(512)S(1)} %get-tuple-element.28, s32[512]{0:T(512)S(1)} %get-tuple-element.27, ...), kind=kOutput, calls=%fused_computation.6 | convolution fusion | flops 278920192 | bytes 9062400 | tf_op jit(solution)/shard_map/qhd,kd->qhk/dot_general | solution.py:100
  91.0 1.3 %fusion.4 = f32[512]{0:T(512)S(1)} fusion(f32[512,2048]{1,0:T(8,128)S(1)} %get-tuple-element.47, f32[512]{0:T(512)S(1)} %get-tuple-element.21, s32[2048]{0:T(1024)S(1)} %fusion.52, s32[512]{0:T(512)S(1)} %get-tuple-element.27), kind=kLoop, calls=%fused_computation.8 | loop fusion | flops 6290944 | bytes 4208640 | tf_op jit(solution)/shard_map/reduce_sum | solution.py:111
  92.3 0.2 bitcast_multiply_fusion
  92.5 1.2 %fusion.11 = f32[512,128]{1,0:T(8,128)S(1)} fusion(f32[512,128]{1,0:T(8,128)S(1)} %get-tuple-element.49, f32[512,2048]{1,0:T(8,128)S(1)} %get-tuple-element.46, f32[512]{0:T(512)S(1)} %get-tuple-element.20, s32[2048]{0:T(1024)S(1)} %fusion.52, s32[512]{0:T(512)S(1)} %get-tuple-element.28, bf16[2048,256]{0,1:T(8,128)(2,1)S(1)} %copy-done.1), kind=kOutput, calls=%fused_computation.14 | convolution fusion | flops 274792448 | bytes 5255168 | tf_op jit(solution)/shard_map/qhk,kd->qhd/dot_general | solution.py:114
  93.7 0.0 copy-start
  93.7 1.2 %fusion.14 = f32[512,128]{1,0:T(8,128)S(1)} fusion(f32[512,128]{1,0:T(8,128)S(1)} %get-tuple-element.48, f32[512,2048]{1,0:T(8,128)S(1)} %get-tuple-element.47, f32[512]{0:T(512)S(1)} %get-tuple-element.21, s32[2048]{0:T(1024)S(1)} %fusion.52, s32[512]{0:T(512)S(1)} %get-tuple-element.27, bf16[2048,256]{0,1:T(8,128)(2,1)S(1)} %copy-done.1), kind=kOutput, calls=%fused_computation.15 | convolution fusion | flops 274792448 | bytes 5255168 | tf_op jit(solution)/shard_map/qhk,kd->qhd/dot_general | solution.py:114
  94.9 0.4 fusion.21
  95.3 0.0 copy-done
  95.3 1.0 %fusion.20 = bf16[1024,128]{1,0:T(8,128)(2,1)} fusion(f32[512,128]{1,0:T(8,128)S(1)} %fusion.14, f32[512,128]{1,0:T(8,128)S(1)} %fusion.11, f32[128]{0:T(128)S(1)} %copy-done, f32[1024]{0:T(1024)S(1)} %add_rsqrt_fusion, f32[1024]{0:T(1024)S(1)} %bitcast.72), kind=kLoop, calls=%fused_computation.24 | loop fusion | flops 655360 | bytes 795136 | tf_op jit(solution)/shard_map/convert_element_type | solution.py:189
  (29 shorter events, 0.3 us)
Async XLA Ops:
  6.5 80.2 %all-gather.2.cloned.1.call-start = ((), (), s32[]{:S(2)}) async-start(), calls=%async_computation | async-start | bytes 1114112 | tf_op jit(solution)/shard_map/all_gather | solution.py:179
  8.2 10.7 %collective-permute-start.1 = (bf16[3,192]{1,0:T(4,128)(2,1)S(1)}, bf16[3,192]{1,0:T(4,128)(2,1)S(1)}, u32[]{:S(2)}, u32[]{:S(2)}) collective-permute-start(bf16[3,192]{1,0:T(4,128)(2,1)S(1)} %pad_maximum_fusion.9), channel_id=1, source_target_pairs={{32,0},{64,32},{96,64},{128,96},{160,128},{192,160},{224,192},{256... | collective-permute-start | bytes 3464 | tf_op jit(solution)/shard_map/ppermute | solution.py:18
  18.8 3.1 %collective-permute-start = (bf16[3,192]{1,0:T(4,128)(2,1)S(1)}, bf16[3,192]{1,0:T(4,128)(2,1)S(1)}, u32[]{:S(2)}, u32[]{:S(2)}) collective-permute-start(bf16[3,192]{1,0:T(4,128)(2,1)S(1)} %get-tuple-element.37), channel_id=1, source_target_pairs={{0,32},{32,64},{64,96},{96,128},{128,160},{160,192},{192,224},{224... | collective-permute-start | bytes 3464 | tf_op jit(solution)/shard_map/ppermute | solution.py:18
  22.6 8.7 %collective-permute-start.2 = (bf16[1152,64]{0,1:T(8,128)(2,1)S(1)}, bf16[1152,64]{0,1:T(8,128)(2,1)S(1)}, u32[]{:S(2)}, u32[]{:S(2)}) collective-permute-start(bf16[1152,64]{0,1:T(8,128)(2,1)S(1)} %pad_maximum_fusion.2), channel_id=1, source_target_pairs={{0,1},{1,0},{2,3},{3,2},{4,5},{5,4},{6,7},{7,6},{8,9},{9,8},{10,11... | collective-permute-start | bytes 442376 | tf_op jit(solution)/shard_map/ppermute | solution.py:28
  31.4 9.4 %collective-permute-start.3 = (bf16[1152,128]{0,1:T(8,128)(2,1)S(1)}, bf16[1152,128]{0,1:T(8,128)(2,1)S(1)}, u32[]{:S(2)}, u32[]{:S(2)}) collective-permute-start(bf16[1152,128]{0,1:T(8,128)(2,1)S(1)} %pad_maximum_fusion), channel_id=1, source_target_pairs={{0,2},{2,0},{1,3},{3,1},{4,6},{6,4},{5,7},{7,5},{8,10},{10,8},{9,1... | collective-permute-start | bytes 884744 | tf_op jit(solution)/shard_map/ppermute | solution.py:28
  86.8 2.1 %copy-start.1 = (bf16[2048,256]{0,1:T(8,128)(2,1)S(1)}, bf16[2048,256]{0,1:T(8,128)(2,1)}, u32[]{:S(2)}) copy-start(bf16[2048,256]{0,1:T(8,128)(2,1)} %all-gather.2.cloned.1.call-done) | copy-start | bytes 3145732
  93.7 1.6 %copy-start = (f32[128]{0:T(128)S(1)}, f32[128]{0:T(128)}, u32[]{:S(2)}) copy-start(f32[128]{0:T(128)} %param.9) | copy-start | bytes 1540
Sparse Core Ops, SparseCore 0:
  41.7 45.0 all-gather.1
where the time goes:
time: 104 us; the launch traced here: 103 us
  waiting for transfers between devices  57 us (55%)
  starting transfers between devices  14.6 us (14%)
  between operations  13.7 us (13%)
  matrix products  7.34 us (7%)
  local copies, waits for them, and re-layouts  6.06 us (6%)
  other arithmetic  4.51 us (4%)
    all_gather x1, waiting for transfers between devices, per_device(): piece = lax.all_gather(packed, 'ctx', axis=0, tiled=True)  43.6 us
    ppermute x2, waiting for transfers between devices, from_partner(): return lax.ppermute(block, axis, route)  12.4 us
    ppermute x2, starting transfers between devices, shifted(): lax.ppermute(value, axis, [(source, source + steps) for source in range(l...  10.7 us
    dot_general x2, matrix products, attend(): jnp.einsum('qhd,kd->qhk', part, keys[:, :HEAD_CHANNELS], preferred_elemen...  4.17 us
    ppermute x2, starting transfers between devices, from_partner(): return lax.ppermute(block, axis, route)  3.84 us
    dot_general x2, matrix products, attend(): jnp.einsum('qhk,kd->qhd', weights.astype(jnp.bfloat16), keys[:, HEAD_CHAN...  2.36 us
  transfers between devices with their start and end apart: 5, of which 4 were waited for; matrix products, arithmetic and copies ran while one was open for 5% of the time, Pallas kernels for 0%

commit v1 on v0

--- a/solution.py
+++ b/solution.py
@@ -176,7 +176,9 @@
     state = local_state(query_heads, pairs, score_scale)
     shard_rows = rows * KEEP // TRANSFORM_BLOCK
     half_rows = shard_rows // 2
-    piece = lax.all_gather(packed, "ctx", axis=0, tiled=True)
+    piece = jnp.concatenate(
+        lax.all_to_all(jnp.stack([packed] * lax.axis_size("ctx")), "ctx", 0, 0), axis=0
+    )
     positions = jnp.arange(piece.shape[0])
     owner = positions // shard_rows
     within = positions % shard_rows

time: 104 us -> 67.8 us (0.65)
  waiting for transfers between devices: 57 us -> 29.8 us
  between operations: 13.7 us -> 0.39 us
  starting transfers between devices: 14.6 us -> 19.9 us
  matrix products: 7.34 us -> 6.14 us
  local copies, waits for them, and re-layouts: 6.06 us -> 7.23 us
    all_gather x1 -> x0, waiting for transfers between devices: 43.6 us -> none  [per_device(): piece = lax.all_gather(packed, 'ctx', axis=0, tiled=True)]
    all_to_all x0 -> x1, waiting for transfers between devices: none -> 15 us  [per_device(): lax.all_to_all(jnp.stack([packed] * lax.axis_size('ctx')), 'ctx', 0, 0)]
    all_to_all x0 -> x1, starting transfers between devices: none -> 5.33 us  [per_device(): lax.all_to_all(jnp.stack([packed] * lax.axis_size('ctx')), 'ctx', 0, 0)]
    ppermute x2, waiting for transfers between devices: 12.4 us -> 13.9 us  [from_partner(): return lax.ppermute(block, axis, route)]
    dot_general x2, matrix products: 4.17 us -> 3.01 us  [attend(): jnp.einsum('qhd,kd->qhk', part, keys[:, :HEAD_CHANNELS], preferred_elemen...]
    another operation x0 -> x1, local copies, waits for them, and re-layouts: none -> 1.07 us  [per_device(): jnp.stack([packed] * lax.axis_size('ctx'))]
  transfers between devices with their start and end apart: 5 -> 5, of which waited for: 4 -> 4; matrix products, arithmetic and copies ran while one was open for 5% -> 7% of each run, Pallas kernels for 0% -> 0%
where the time goes in v1:
time: 67.8 us; the launch traced here: 67.4 us
  waiting for transfers between devices  29.8 us (44%)
  starting transfers between devices  19.9 us (29%)
  local copies, waits for them, and re-layouts  7.23 us (11%)
  matrix products  6.14 us (9%)
  other arithmetic  3.88 us (6%)
    all_to_all x1, waiting for transfers between devices, per_device(): lax.all_to_all(jnp.stack([packed] * lax.axis_size('ctx')), 'ctx', 0, 0)  15 us
    ppermute x2, waiting for transfers between devices, from_partner(): return lax.ppermute(block, axis, route)  13.9 us
    ppermute x2, starting transfers between devices, shifted(): lax.ppermute(value, axis, [(source, source + steps) for source in range(l...  10.7 us
    all_to_all x1, starting transfers between devices, per_device(): lax.all_to_all(jnp.stack([packed] * lax.axis_size('ctx')), 'ctx', 0, 0)  5.33 us
    ppermute x2, starting transfers between devices, from_partner(): return lax.ppermute(block, axis, route)  3.84 us
    dot_general x2, matrix products, attend(): jnp.einsum('qhd,kd->qhk', part, keys[:, :HEAD_CHANNELS], preferred_elemen...  3.01 us
    dot_general x2, matrix products, attend(): jnp.einsum('qhk,kd->qhd', weights.astype(jnp.bfloat16), keys[:, HEAD_CHAN...  2.34 us
    mul x2, local copies, waits for them, and re-layouts, causal_conv(): total = weights[0] * values.astype(jnp.float32)  1.67 us
  transfers between devices with their start and end apart: 5, of which 4 were waited for; matrix products, arithmetic and copies ran while one was open for 7% of the time, Pallas kernels for 0%

profile of v1, /device:TPU:1, one launch (start us, length us, event | category | flops | bytes accessed | tf_op | source)
XLA Modules:
  0.0 67.4 jit_solution(18118026835854042903)
XLA Ops:
  0.0 0.7 %fusion.93 = (bf16[3,128]{1,0:T(4,128)(2,1)S(1)}, bf16[3,128]{1,0:T(4,128)(2,1)S(1)}) fusion(bf16[1024,128]{1,0:T(8,128)(2,1)} %param.5), kind=kLoop, calls=%fused_computation.168 | loop fusion | bytes 3072 | tf_op jit(solution)/shard_map/slice | solution.py:136
  0.7 0.8 %fusion.95 = (bf16[3,64]{0,1:T(8,128)(2,1)S(1)}, bf16[3,64]{0,1:T(8,128)(2,1)S(1)}) fusion(bf16[1024,64]{0,1:T(8,128)(2,1)} %param.6), kind=kLoop, calls=%fused_computation.170 | loop fusion | bytes 1536 | tf_op jit(solution)/shard_map/slice | solution.py:136
  1.5 0.1 copy.43
  1.6 8.8 %collective-permute-start.1 = (bf16[3,192]{1,0:T(4,128)(2,1)S(1)}, bf16[3,192]{1,0:T(4,128)(2,1)S(1)}, u32[]{:S(2)}, u32[]{:S(2)}) collective-permute-start(bf16[3,192]{1,0:T(4,128)(2,1)S(1)} %pad_maximum_fusion.9), channel_id=1, source_target_pairs={{32,0},{64,32},{96,64},{128,96},{160,128},{192,160},{224,192},{256... | collective-permute-start | bytes 3464 | tf_op jit(solution)/shard_map/ppermute | solution.py:18
  10.4 0.9 %fusion.94 = (bf16[512,64]{0,1:T(8,128)(2,1)S(1)}, bf16[512,64]{0,1:T(8,128)(2,1)S(1)}) fusion(bf16[1024,64]{0,1:T(8,128)(2,1)} %param.6), kind=kLoop, calls=%fused_computation.169 | loop fusion | bytes 262144 | tf_op jit(solution)/shard_map/slice | solution.py:151
  11.3 1.0 %fusion.92 = (bf16[512,128]{1,0:T(8,128)(2,1)S(1)}, bf16[512,128]{1,0:T(8,128)(2,1)S(1)}) fusion(bf16[1024,128]{1,0:T(8,128)(2,1)} %param.5), kind=kLoop, calls=%fused_computation.167 | loop fusion | bytes 524288 | tf_op jit(solution)/shard_map/slice | solution.py:144
  12.3 0.8 %slice_bitcast_fusion.7 = (f32[128]{0:T(128)S(1)}, f32[128]{0:T(128)S(1)}, f32[128]{0:T(128)S(1)}, f32[128]{0:T(128)S(1)}) fusion(f32[4,128]{1,0:T(4,128)} %param.7), kind=kLoop, calls=%fused_computation.154 | loop fusion | bytes 4096 | tf_op jit(solution)/shard_map/mul | solution.py:51
  13.1 0.8 %slice_bitcast_fusion.3 = (f32[64]{0:T(128)S(1)}, f32[64]{0:T(128)S(1)}, f32[64]{0:T(128)S(1)}, f32[64]{0:T(128)S(1)}) fusion(f32[4,64]{1,0:T(4,128)} %param.8), kind=kLoop, calls=%fused_computation.150 | loop fusion | bytes 2048 | tf_op jit(solution)/shard_map/mul | solution.py:51
  14.0 0.1 copy.42
  14.1 0.0 collective-permute-done.1
  14.1 1.9 %collective-permute-start = (bf16[3,192]{1,0:T(4,128)(2,1)S(1)}, bf16[3,192]{1,0:T(4,128)(2,1)S(1)}, u32[]{:S(2)}, u32[]{:S(2)}) collective-permute-start(bf16[3,192]{1,0:T(4,128)(2,1)S(1)} %get-tuple-element.37), channel_id=1, source_target_pairs={{0,32},{32,64},{64,96},{96,128},{128,160},{160,192},{192,224},{224... | collective-permute-start | bytes 3464 | tf_op jit(solution)/shard_map/ppermute | solution.py:18
  16.1 0.1 copy.32
  16.2 1.0 %collective-permute-done = bf16[3,192]{1,0:T(4,128)(2,1)S(1)} collective-permute-done((bf16[3,192]{1,0:T(4,128)(2,1)S(1)}, bf16[3,192]{1,0:T(4,128)(2,1)S(1)}, u32[]{:S(2)}, u32[]{:S(2)}) %collective-permute-start) | collective-permute-done | bytes 1184 | tf_op jit(solution)/shard_map/ppermute | solution.py:18
  17.2 0.1 copy.31
  17.3 0.2 add_convert_fusion.3
  17.5 0.2 convolution_convert_fusion
  17.7 0.1 copy.34
  17.9 1.9 %collective-permute-start.2 = (bf16[1152,64]{0,1:T(8,128)(2,1)S(1)}, bf16[1152,64]{0,1:T(8,128)(2,1)S(1)}, u32[]{:S(2)}, u32[]{:S(2)}) collective-permute-start(bf16[1152,64]{0,1:T(8,128)(2,1)S(1)} %pad_maximum_fusion.2), channel_id=1, source_target_pairs={{0,1},{1,0},{2,3},{3,2},{4,5},{5,4},{6,7},{7,6},{8,9},{9,8},{10,11... | collective-permute-start | bytes 442376 | tf_op jit(solution)/shard_map/ppermute | solution.py:28
  19.9 6.7 %collective-permute-done.2 = bf16[1152,64]{0,1:T(8,128)(2,1)S(1)} collective-permute-done((bf16[1152,64]{0,1:T(8,128)(2,1)S(1)}, bf16[1152,64]{0,1:T(8,128)(2,1)S(1)}, u32[]{:S(2)}, u32[]{:S(2)}) %collective-permute-start.2) | collective-permute-done | bytes 147488 | tf_op jit(solution)/shard_map/ppermute | solution.py:28
  26.6 0.1 maximum_select_fusion.1
  26.7 1.9 %collective-permute-start.3 = (bf16[1152,128]{0,1:T(8,128)(2,1)S(1)}, bf16[1152,128]{0,1:T(8,128)(2,1)S(1)}, u32[]{:S(2)}, u32[]{:S(2)}) collective-permute-start(bf16[1152,128]{0,1:T(8,128)(2,1)S(1)} %pad_maximum_fusion), channel_id=1, source_target_pairs={{0,2},{2,0},{1,3},{3,1},{4,6},{6,4},{5,7},{7,5},{8,10},{10,8},{9,1... | collective-permute-start | bytes 884744 | tf_op jit(solution)/shard_map/ppermute | solution.py:28
  28.7 0.3 add_convert_fusion.1
  29.0 7.2 %collective-permute-done.3 = bf16[1152,128]{0,1:T(8,128)(2,1)S(1)} collective-permute-done((bf16[1152,128]{0,1:T(8,128)(2,1)S(1)}, bf16[1152,128]{0,1:T(8,128)(2,1)S(1)}, u32[]{:S(2)}, u32[]{:S(2)}) %collective-permute-start.3) | collective-permute-done | bytes 294944 | tf_op jit(solution)/shard_map/ppermute | solution.py:28
  36.2 0.1 maximum_select_fusion
  36.4 0.1 copy.38
  36.5 0.2 copy.37
  36.7 1.1 %stack.2 = bf16[16,128,256]{2,1,0:T(8,128)(2,1)} broadcast(bf16[128,256]{1,0:T(8,128)(2,1)S(1)} %copy.38), dimensions={1,2} | broadcast | bytes 1114112 | tf_op jit(solution)/shard_map/stack | solution.py:180
  37.8 5.3 %all-to-all-start = ((bf16[16,128,256]{2,1,0:T(8,128)(2,1)}), bf16[16,128,256]{2,1,0:T(8,128)(2,1)S(1)}, u32[]{:S(2)}, u32[]{:S(2)}) async-start(bf16[16,128,256]{2,1,0:T(8,128)(2,1)} %stack.2), calls=%async_computation | async-start | bytes 2097152 | tf_op jit(solution)/shard_map/all_to_all | solution.py:180
  43.1 0.3 fusion.99
  43.4 0.1 fusion.28
  43.5 0.2 copy.39
  43.7 0.3 fusion.30
  44.1 15.0 %all-to-all-done = bf16[16,128,256]{2,1,0:T(8,128)(2,1)S(1)} async-done(((bf16[16,128,256]{2,1,0:T(8,128)(2,1)}), bf16[16,128,256]{2,1,0:T(8,128)(2,1)S(1)}, u32[]{:S(2)}, u32[]{:S(2)}) %all-to-all-start) | async-done | bytes 1048608 | tf_op jit(solution)/shard_map/all_to_all | solution.py:180
  59.0 0.9 %fusion = (f32[512]{0:T(512)S(1)}, f32[512,2048]{1,0:T(8,128)S(1)}) fusion(s32[2048]{0:T(1024)S(1)} %fusion.52, s32[512]{0:T(512)S(1)} %get-tuple-element.28, bf16[512,128]{1,0:T(8,128)(2,1)S(1)} %get-tuple-element.29, bf16[2048,256]{1,0:T(8,128)(2,1)S(1)} %bitcast.67), kind=kOutput, calls=%fused_computation.4 | convolution fusion | flops 272629248 | bytes 4861952 | tf_op jit(solution)/shard_map/qhd,kd->qhk/dot_general | solution.py:100
  60.0 2.1 %fusion.2 = (f32[512]{0:T(512)S(1)}, f32[512]{0:T(512)S(1)}, f32[512,2048]{1,0:T(8,128)S(1)}) fusion(f32[512,2048]{1,0:T(8,128)S(1)} %get-tuple-element.46, f32[512]{0:T(512)S(1)} %get-tuple-element.20, s32[2048]{0:T(1024)S(1)} %fusion.52, s32[512]{0:T(512)S(1)} %get-tuple-element.28, s32[512]{0:T(512)S(1)} %get-tuple-element.27, ...), kind=kOutput, calls=%fused_computation.6 | convolution fusion | flops 278920192 | bytes 9062400 | tf_op jit(solution)/shard_map/qhd,kd->qhk/dot_general | solution.py:100
  62.1 0.2 bitcast_multiply_fusion
  62.3 1.2 %fusion.11 = f32[512,128]{1,0:T(8,128)S(1)} fusion(f32[512,128]{1,0:T(8,128)S(1)} %get-tuple-element.49, f32[512,2048]{1,0:T(8,128)S(1)} %get-tuple-element.46, f32[512]{0:T(512)S(1)} %get-tuple-element.20, s32[2048]{0:T(1024)S(1)} %fusion.52, s32[512]{0:T(512)S(1)} %get-tuple-element.28, bf16[2048,256]{1,0:T(8,128)(2,1)S(1)} %bitcast.69), kind=kOutput, calls=%fused_computation.14 | convolution fusion | flops 274792448 | bytes 5255168 | tf_op jit(solution)/shard_map/qhk,kd->qhd/dot_general | solution.py:114
  63.5 1.2 %fusion.4 = f32[512]{0:T(512)S(1)} fusion(f32[512,2048]{1,0:T(8,128)S(1)} %get-tuple-element.47, f32[512]{0:T(512)S(1)} %get-tuple-element.21, s32[2048]{0:T(1024)S(1)} %fusion.52, s32[512]{0:T(512)S(1)} %get-tuple-element.27), kind=kLoop, calls=%fused_computation.8 | loop fusion | flops 6290944 | bytes 4208640 | tf_op jit(solution)/shard_map/reduce_sum | solution.py:111
  64.7 0.0 copy-start
  64.7 1.2 %fusion.14 = f32[512,128]{1,0:T(8,128)S(1)} fusion(f32[512,128]{1,0:T(8,128)S(1)} %get-tuple-element.48, f32[512,2048]{1,0:T(8,128)S(1)} %get-tuple-element.47, f32[512]{0:T(512)S(1)} %get-tuple-element.21, s32[2048]{0:T(1024)S(1)} %fusion.52, s32[512]{0:T(512)S(1)} %get-tuple-element.27, bf16[2048,256]{1,0:T(8,128)(2,1)S(1)} %bitcast.70), kind=kOutput, calls=%fused_computation.15 | convolution fusion | flops 274792448 | bytes 5255168 | tf_op jit(solution)/shard_map/qhk,kd->qhd/dot_general | solution.py:114
  65.9 0.4 fusion.21
  66.3 0.0 copy-done
  66.3 1.0 %fusion.20 = bf16[1024,128]{1,0:T(8,128)(2,1)} fusion(f32[512,128]{1,0:T(8,128)S(1)} %fusion.14, f32[512,128]{1,0:T(8,128)S(1)} %fusion.11, f32[128]{0:T(128)S(1)} %copy-done, f32[1024]{0:T(1024)S(1)} %add_rsqrt_fusion, f32[1024]{0:T(1024)S(1)} %bitcast.77), kind=kLoop, calls=%fused_computation.24 | loop fusion | flops 655360 | bytes 795136 | tf_op jit(solution)/shard_map/convert_element_type | solution.py:191
  (30 shorter events, 0.4 us)
Async XLA Ops:
  1.6 12.5 %collective-permute-start.1 = (bf16[3,192]{1,0:T(4,128)(2,1)S(1)}, bf16[3,192]{1,0:T(4,128)(2,1)S(1)}, u32[]{:S(2)}, u32[]{:S(2)}) collective-permute-start(bf16[3,192]{1,0:T(4,128)(2,1)S(1)} %pad_maximum_fusion.9), channel_id=1, source_target_pairs={{32,0},{64,32},{96,64},{128,96},{160,128},{192,160},{224,192},{256... | collective-permute-start | bytes 3464 | tf_op jit(solution)/shard_map/ppermute | solution.py:18
  14.1 3.1 %collective-permute-start = (bf16[3,192]{1,0:T(4,128)(2,1)S(1)}, bf16[3,192]{1,0:T(4,128)(2,1)S(1)}, u32[]{:S(2)}, u32[]{:S(2)}) collective-permute-start(bf16[3,192]{1,0:T(4,128)(2,1)S(1)} %get-tuple-element.37), channel_id=1, source_target_pairs={{0,32},{32,64},{64,96},{96,128},{128,160},{160,192},{192,224},{224... | collective-permute-start | bytes 3464 | tf_op jit(solution)/shard_map/ppermute | solution.py:18
  17.9 8.7 %collective-permute-start.2 = (bf16[1152,64]{0,1:T(8,128)(2,1)S(1)}, bf16[1152,64]{0,1:T(8,128)(2,1)S(1)}, u32[]{:S(2)}, u32[]{:S(2)}) collective-permute-start(bf16[1152,64]{0,1:T(8,128)(2,1)S(1)} %pad_maximum_fusion.2), channel_id=1, source_target_pairs={{0,1},{1,0},{2,3},{3,2},{4,5},{5,4},{6,7},{7,6},{8,9},{9,8},{10,11... | collective-permute-start | bytes 442376 | tf_op jit(solution)/shard_map/ppermute | solution.py:28
  26.7 9.4 %collective-permute-start.3 = (bf16[1152,128]{0,1:T(8,128)(2,1)S(1)}, bf16[1152,128]{0,1:T(8,128)(2,1)S(1)}, u32[]{:S(2)}, u32[]{:S(2)}) collective-permute-start(bf16[1152,128]{0,1:T(8,128)(2,1)S(1)} %pad_maximum_fusion), channel_id=1, source_target_pairs={{0,2},{2,0},{1,3},{3,1},{4,6},{6,4},{5,7},{7,5},{8,10},{10,8},{9,1... | collective-permute-start | bytes 884744 | tf_op jit(solution)/shard_map/ppermute | solution.py:28
  37.8 21.3 %all-to-all-start = ((bf16[16,128,256]{2,1,0:T(8,128)(2,1)}), bf16[16,128,256]{2,1,0:T(8,128)(2,1)S(1)}, u32[]{:S(2)}, u32[]{:S(2)}) async-start(bf16[16,128,256]{2,1,0:T(8,128)(2,1)} %stack.2), calls=%async_computation | async-start | bytes 2097152 | tf_op jit(solution)/shard_map/all_to_all | solution.py:180
  64.7 1.6 %copy-start = (f32[128]{0:T(128)S(1)}, f32[128]{0:T(128)}, u32[]{:S(2)}) copy-start(f32[128]{0:T(128)} %param.9) | copy-start | bytes 1540
